TPU v7x, 32 devices: a whole 2x2x4 slice. The times are simulated.
32 devices in a mesh: dom: 8 (over z, core), leaf: 4 (over y, x).
Axes of the slice: x: 2, y: 2, z: 4, core: 2. Of those that a mesh axis runs over, the one named last changes fastest.
Arguments:
- sources: bfloat16 [32, 196608], P(None, ('dom', 'leaf')), may hold values from -6 to 6
- points: bfloat16 [3, 196608], P(None, ('dom', 'leaf')), may hold values from -4 to 4
- basis: bfloat16 [768, 64, 256], P(('dom', 'leaf')), may hold values from -0.375 to 0.375
- transfer_one: bfloat16 [768, 4096], P(('dom', 'leaf')), may hold values from -0.5 to 0.5
- transfer_two: bfloat16 [384, 4096], P(('dom', 'leaf')), may hold values from -0.5 to 0.5
- near_list: int32 [768, 16], P(('dom', 'leaf')), may hold values from -1 to 767, as said below
- couple_zero: bfloat16 [768, 32, 4096], P(('dom', 'leaf')), may hold values from -0.125 to 0.125
- couple_one: bfloat16 [384, 32, 4096], P(('dom', 'leaf')), may hold values from -0.125 to 0.125
- couple_two: bfloat16 [192, 32, 4096], P(('dom', 'leaf')), may hold values from -0.125 to 0.125
- list_zero: int32 [768, 32], P(('dom', 'leaf')), may hold values from -1 to 767, as said below
- list_one: int32 [384, 32], P(('dom', 'leaf')), may hold values from -1 to 383, as said below
- list_two: int32 [192, 32], P(('dom', 'leaf')), may hold values from -1 to 191, as said below
Outputs:
- product: bfloat16 [32, 196608], P(None, ('dom', 'leaf'))
Inputs may be any that keep to these rules, and one draw needn't show every extreme that they name: `near_list`: row b holds leaf b itself first, then distinct other leaves within 24 positions of b; -1 marks empty slots, which come last. `list_zero`: row b holds distinct leaves other than b whose subdomain differs from b's by at most one, a subdomain being the leaves of one index of the dom axis; -1 marks empty slots, which come last. `list_one`: as for list_zero, with the boxes of level one. `list_two`: as for list_zero, with the boxes of level two.
All inputs are finite; a program needn't handle non-finite values.
Results may differ from a plain program's by a relative error of at most 0.0061.
Values may be sent and summed in bfloat16 or wider, within the bound.
No kernel may reach another device: no remote copies, remote signals or barrier semaphores. Data moves between devices by JAX's collectives and lax.ppermute only.
A program may use at most 128 MiB of HBM per device.

v0:
```python
import math

import jax
import jax.numpy as jnp
from jax import lax
from jax.sharding import PartitionSpec as P

delta_sq = 0.01


def extended_2(cells, sides, width):
    for axis, dim in sides:
        count = lax.axis_size(axis)
        ends = count - 1
        head = lax.slice_in_dim(cells, 0, width, axis=dim)
        tail = lax.slice_in_dim(cells, cells.shape[dim] - width, cells.shape[dim], axis=dim)
        cells = jnp.concatenate(
            [
                lax.ppermute(tail, axis, [(i, (i + 1) % count) for i in range(ends)]),
                cells,
                lax.ppermute(head, axis, [((i + 1) % count, i) for i in range(ends)]),
            ],
            axis=dim,
        )
    return cells


def fetch_group(coeff_level):
    boxes = coeff_level.shape[0]
    rows = coeff_level.reshape(boxes, -1)
    joined = lax.all_gather(rows, "leaf", axis=0, tiled=True)
    widened = extended_2(joined, (("dom", 0),), joined.shape[0])
    return widened


def couple_local(fetched, matrices, lists, first_box, right_count, rank_size):
    boxes = lists.shape[0]
    slot_count = lists.shape[1]
    is_valid = lists >= 0
    local_index = jnp.where(is_valid, lists - first_box, 0)
    picked = jnp.take(fetched, local_index.reshape(-1), axis=0)
    picked = picked.reshape(boxes, slot_count, right_count, rank_size)
    picked = picked * is_valid.astype(jnp.bfloat16)[:, :, None, None]
    blocks = matrices.reshape(boxes, slot_count, rank_size, rank_size)
    return jnp.einsum("bsrj,bskj->brk", picked, blocks, preferred_element_type=jnp.float32)


def upward(lower, transfer):
    boxes = lower.shape[0] // 2
    right_count = lower.shape[1]
    rank_size = lower.shape[2]
    children = lower.reshape(boxes, 2, right_count, rank_size)
    matrices = transfer.reshape(boxes, 2, rank_size, rank_size)
    return jnp.einsum(
        "bcrj,bckj->brk", children, matrices, preferred_element_type=jnp.float32
    ).astype(jnp.bfloat16)


def downward(far_terms, upper, transfer):
    boxes = upper.shape[0]
    right_count = upper.shape[1]
    rank_size = upper.shape[2]
    matrices = transfer.reshape(boxes, 2, rank_size, rank_size)
    spread_down = jnp.einsum("brk,bckj->bcrj", upper, matrices, preferred_element_type=jnp.float32)
    return (far_terms + spread_down.reshape(2 * boxes, right_count, rank_size)).astype(jnp.bfloat16)


def shards(
    sources,
    points,
    basis,
    transfer_one,
    transfer_two,
    near_list,
    couple_zero,
    couple_one,
    couple_two,
    list_zero,
    list_one,
    list_two,
):
    right_count = sources.shape[0]
    leaves = basis.shape[0]
    rank_size = basis.shape[1]
    leaf_width = basis.shape[2]
    members = lax.axis_size("leaf")
    group_index = lax.axis_index("dom")
    device = group_index * members + lax.axis_index("leaf")
    stacked = jnp.concatenate([sources, points], axis=0)
    extended = extended_2(stacked, ((("dom", "leaf"), 1),), leaves * leaf_width)
    first_leaf = (device - 1) * leaves
    span_count = extended.shape[1] // leaf_width
    ext_rows = jnp.transpose(extended.reshape(right_count + 3, span_count, leaf_width), (1, 0, 2))
    ext_values = ext_rows[:, :right_count, :]
    ext_coords = ext_rows[:, right_count:, :].astype(jnp.float32)
    own_leaf = device * leaves + jnp.arange(leaves, dtype=jnp.int32)
    is_valid = near_list >= 0
    local_index = jnp.where(is_valid, near_list, own_leaf[:, None]) - first_leaf
    own_coords = ext_coords[leaves : 2 * leaves]
    scale_factor = 1.0 / math.sqrt(near_list.shape[1] * leaf_width)

    def near_one(leaf_item):
        slot_ids, slot_mask, target = leaf_item
        source = jnp.take(ext_coords, slot_ids, axis=0)
        distance = jnp.zeros((leaf_width, slot_ids.shape[0], leaf_width), jnp.float32)
        for component in range(3):
            difference = target[component][:, None, None] - source[:, component, :][None, :, :]
            distance = distance + difference * difference
        kernel = (
            scale_factor
            * lax.rsqrt(distance + delta_sq)
            * slot_mask.astype(jnp.float32)[None, :, None]
        )
        kernel = kernel.astype(jnp.bfloat16)
        gathered = jnp.take(ext_values, slot_ids, axis=0)
        return lax.dot_general(
            gathered, kernel, (((0, 2), (1, 2)), ((), ())), preferred_element_type=jnp.float32
        )

    near_terms = lax.map(near_one, (local_index, is_valid, own_coords))
    values = sources.reshape(right_count, leaves, leaf_width)
    level_zero = jnp.einsum(
        "rbp,bkp->brk", values, basis, preferred_element_type=jnp.float32
    ).astype(jnp.bfloat16)
    level_one = upward(level_zero, transfer_one)
    level_two = upward(level_one, transfer_two)
    levels_all = (level_zero, level_one, level_two)
    fetched = [fetch_group(coeff_level) for coeff_level in levels_all]
    first_zero = (group_index - 1) * members * leaves
    first_one = (group_index - 1) * members * (leaves // 2)
    first_two = (group_index - 1) * members * (leaves // 4)
    far_zero = couple_local(fetched[0], couple_zero, list_zero, first_zero, right_count, rank_size)
    far_one = couple_local(fetched[1], couple_one, list_one, first_one, right_count, rank_size)
    far_two = couple_local(fetched[2], couple_two, list_two, first_two, right_count, rank_size)
    down_two = far_two.astype(jnp.bfloat16)
    down_one = downward(far_one, down_two, transfer_two)
    down_zero = downward(far_zero, down_one, transfer_one)
    far_part = jnp.einsum("brk,bkp->brp", down_zero, basis, preferred_element_type=jnp.float32)
    total = near_terms + far_part
    return jnp.transpose(total, (1, 0, 2)).reshape(right_count, -1).astype(jnp.bfloat16)


def solution(mesh):
    placed = (
        P(None, ("dom", "leaf")),
        P(None, ("dom", "leaf")),
        P(("dom", "leaf"), None, None),
        P(("dom", "leaf"), None),
        P(("dom", "leaf"), None),
        P(("dom", "leaf"), None),
        P(("dom", "leaf"), None, None),
        P(("dom", "leaf"), None, None),
        P(("dom", "leaf"), None, None),
        P(("dom", "leaf"), None),
        P(("dom", "leaf"), None),
        P(("dom", "leaf"), None),
    )
    return jax.shard_map(
        shards, mesh=mesh, in_specs=placed, out_specs=P(None, ("dom", "leaf")), check_vma=False
    )
```

profile of v0, /device:TPU:11, one launch (start us, length us, event | category | flops | bytes accessed | tf_op | source)
XLA Modules:
  0.0 232.7 jit_solution(17080197640222384998)
XLA Ops:
  2.6 1.5 convolution_convert_fusion
  4.6 6.5 %all-gather.1 = bf16[4,6,2048]{2,1,0:T(8,128)(2,1)S(1)} all-gather(bf16[1,6,2048]{2,1,0:T(8,128)(2,1)S(1)} %reshape.295), channel_id=1, replica_groups=mesh['dom'=8,'leaf'=4] {'leaf'}, dimensions={0}, use_global_device_ids=true | all-gather | bytes 122880 | tf_op jit(solution)/shard_map/all_gather | solution.py:31
  11.1 4.6 %collective-permute-start.7 = (bf16[24,2048]{1,0:T(8,128)(2,1)S(1)}, bf16[24,2048]{1,0:T(8,128)(2,1)S(1)}, u32[]{:S(2)}, u32[]{:S(2)}) collective-permute-start(bf16[24,2048]{1,0:T(8,128)(2,1)S(1)} %reshape.296), channel_id=1, source_target_pairs={{4,0},{8,4},{12,8},{16,12},{20,16},{24,20},{28,24},{5,1},{9,5},{13... | collective-permute-start | bytes 294920 | tf_op jit(solution)/shard_map/ppermute | solution.py:21
  15.7 3.1 %collective-permute-start.6 = (bf16[24,2048]{1,0:T(8,128)(2,1)S(1)}, bf16[24,2048]{1,0:T(8,128)(2,1)}, u32[]{:S(2)}, u32[]{:S(2)}) collective-permute-start(bf16[24,2048]{1,0:T(8,128)(2,1)S(1)} %reshape.296), channel_id=1, source_target_pairs={{0,4},{4,8},{8,12},{12,16},{16,20},{20,24},{24,28},{1,5},{5,9},{9,... | collective-permute-start | bytes 294920 | tf_op jit(solution)/shard_map/ppermute | solution.py:19
  19.0 6.7 %all-gather = bf16[4,12,2048]{2,1,0:T(8,128)(2,1)S(1)} all-gather(bf16[1,12,2048]{2,1,0:T(8,128)(2,1)S(1)} %reshape.293), channel_id=1, replica_groups=mesh['dom'=8,'leaf'=4] {'leaf'}, dimensions={0}, use_global_device_ids=true | all-gather | bytes 245760 | tf_op jit(solution)/shard_map/all_gather | solution.py:31
  25.8 2.8 %collective-permute-start.5 = (bf16[48,2048]{1,0:T(8,128)(2,1)S(1)}, bf16[48,2048]{1,0:T(8,128)(2,1)S(1)}, u32[]{:S(2)}, u32[]{:S(2)}) collective-permute-start(bf16[48,2048]{1,0:T(8,128)(2,1)S(1)} %reshape.294), channel_id=1, source_target_pairs={{4,0},{8,4},{12,8},{16,12},{20,16},{24,20},{28,24},{5,1},{9,5},{13... | collective-permute-start | bytes 589832 | tf_op jit(solution)/shard_map/ppermute | solution.py:21
  28.6 3.1 %collective-permute-start.4 = (bf16[48,2048]{1,0:T(8,128)(2,1)S(1)}, bf16[48,2048]{1,0:T(8,128)(2,1)S(1)}, u32[]{:S(2)}, u32[]{:S(2)}) collective-permute-start(bf16[48,2048]{1,0:T(8,128)(2,1)S(1)} %reshape.294), channel_id=1, source_target_pairs={{0,4},{4,8},{8,12},{12,16},{16,20},{20,24},{24,28},{1,5},{5,9},{9,... | collective-permute-start | bytes 589832 | tf_op jit(solution)/shard_map/ppermute | solution.py:19
  31.9 9.3 %all_gather.9 = bf16[96,2048]{1,0:T(8,128)(2,1)} all-gather(bf16[24,2048]{1,0:T(8,128)(2,1)S(1)} %reshape.238), channel_id=1, replica_groups=mesh['dom'=8,'leaf'=4] {'leaf'}, dimensions={0}, use_global_device_ids=true | all-gather | bytes 491520 | tf_op jit(solution)/shard_map/all_gather | solution.py:31
  41.2 2.8 %collective-permute-start.3 = (bf16[96,2048]{1,0:T(8,128)(2,1)}, bf16[96,2048]{1,0:T(8,128)(2,1)}, u32[]{:S(2)}, u32[]{:S(2)}) collective-permute-start(bf16[96,2048]{1,0:T(8,128)(2,1)} %all_gather.9), channel_id=1, source_target_pairs={{4,0},{8,4},{12,8},{16,12},{20,16},{24,20},{28,24},{5,1},{9,5},{13... | collective-permute-start | bytes 1179656 | tf_op jit(solution)/shard_map/ppermute | solution.py:21
  46.9 5.5 %reshape.250 = bf16[6,32,64,64]{3,2,1,0:T(8,128)(2,1)} reshape(bf16[6,32,4096]{2,1,0:T(8,128)(2,1)} %param.22) | data formatting | bytes 3145728 | tf_op jit(solution)/shard_map/reshape | solution.py:44
  52.5 9.6 %reshape.245 = bf16[12,32,64,64]{3,2,1,0:T(8,128)(2,1)} reshape(bf16[12,32,4096]{2,1,0:T(8,128)(2,1)} %param.21) | data formatting | bytes 6291456 | tf_op jit(solution)/shard_map/reshape | solution.py:44
  62.1 17.9 %reshape.240 = bf16[24,32,64,64]{3,2,1,0:T(8,128)(2,1)} reshape(bf16[24,32,4096]{2,1,0:T(8,128)(2,1)} %param.20) | data formatting | bytes 12582912 | tf_op jit(solution)/shard_map/reshape | solution.py:44
  80.2 3.1 %collective-permute-start.2 = (bf16[96,2048]{1,0:T(8,128)(2,1)}, bf16[96,2048]{1,0:T(8,128)(2,1)}, u32[]{:S(2)}, u32[]{:S(2)}) collective-permute-start(bf16[96,2048]{1,0:T(8,128)(2,1)} %all_gather.9), channel_id=1, source_target_pairs={{0,4},{4,8},{8,12},{12,16},{16,20},{20,24},{24,28},{1,5},{5,9},{9,... | collective-permute-start | bytes 1179656 | tf_op jit(solution)/shard_map/ppermute | solution.py:19
  83.4 2.1 collective-permute-start.1
  87.5 2.5 %gather.31 = bf16[6,32,32,64]{3,2,1,0:T(8,128)(2,1)} reshape(bf16[192,2048]{1,0:T(8,128)(2,1)S(1)} %gather_fusion.4) | data formatting | bytes 1572864 | tf_op jit(solution)/shard_map/jit(_take)/gather | solution.py:41
  90.1 4.2 %fusion.64 = f32[6,32,2,64]{3,1,2,0:T(8,128)} fusion(bf16[6,2,64,64]{3,2,1,0:T(8,128)(2,1)S(1)} %reshape.247, bf16[6,32,64,64]{3,2,1,0:T(8,128)(2,1)} %reshape.250, bf16[6,32,32,64]{3,2,1,0:T(8,128)(2,1)} %gather.31, pred[6,32]{1,0:T(8,128)(4,1)S(1)} %get-tuple-element.75, bf16[6,32]{1,0:T(8,128)(2,1)S(1)} %get-tuple-element.87), kind=kOutput, calls=%fused_computation.67 | convolution fusion | flops 54276096 | bytes 2556480 | tf_op jit(solution)/shard_map/brk,bckj->bcrj/dot_general | solution.py:64
  94.3 4.2 %collective-permute-start = (bf16[35,6144]{1,0:T(8,128)(2,1)S(1)}, bf16[35,6144]{1,0:T(8,128)(2,1)}, u32[]{:S(2)}, u32[]{:S(2)}) collective-permute-start(bf16[35,6144]{1,0:T(8,128)(2,1)S(1)} %constant_dynamic-update-slice_fusion), channel_id=1, source_target_pairs={{0,1},{1,2},{2,3},{3,4},{4,5},{5,6},{6,7},{7,8},{8,9},{9,10},{10,1... | collective-permute-start | bytes 1290248 | tf_op jit(solution)/shard_map/ppermute | solution.py:19
  98.6 2.5 %gather_fusion.3 = bf16[384,2048]{1,0:T(8,128)(2,1)S(1)} fusion(bf16[144,2048]{1,0:T(8,128)(2,1)S(1)} %pad_maximum_fusion.2, s32[1024]{0:T(1024)S(1)} %copy-done.6), kind=kCustom, calls=%fused_computation.3 | custom fusion | bytes 3147264 | tf_op jit(solution)/shard_map/jit(_take)/gather | solution.py:41
  101.1 4.2 %gather.29 = bf16[12,32,32,64]{3,2,1,0:T(8,128)(2,1)} reshape(bf16[384,2048]{1,0:T(8,128)(2,1)S(1)} %gather_fusion.3) | data formatting | bytes 3145728 | tf_op jit(solution)/shard_map/jit(_take)/gather | solution.py:41
  105.4 5.6 %fusion.51 = f32[12,32,2,64]{3,1,2,0:T(8,128)} fusion(bf16[12,2,64,64]{3,2,1,0:T(8,128)(2,1)S(1)} %copy-done.3, f32[12,32,64]{2,1,0:T(8,128)S(1)} %bitcast.144, bf16[12,32,64,64]{3,2,1,0:T(8,128)(2,1)} %reshape.245, bf16[12,32,32,64]{3,2,1,0:T(8,128)(2,1)} %gather.29, pred[12,32]{1,0:T(8,128)(4,1)S(1)} %copy-done.13, bf16[12,32]{1,0:T(8,128)(2,1)S(1)} %copy-done.11), kind=kOutput, calls=%fused_computation.61 | convolution fusion | flops 108576768 | bytes 5211264 | tf_op jit(solution)/shard_map/brk,bckj->bcrj/dot_general | solution.py:64
  112.3 4.3 %gather_fusion.2 = bf16[768,2048]{1,0:T(8,128)(2,1)} fusion(bf16[288,2048]{1,0:T(8,128)(2,1)S(1)} %pad_maximum_fusion.1, s32[1024]{0:T(1024)S(1)} %pad_clamp_fusion.3), kind=kCustom, calls=%fused_computation.2 | custom fusion | bytes 6294528 | tf_op jit(solution)/shard_map/jit(_take)/gather | solution.py:41
  116.6 10.1 %gather.27 = bf16[24,32,32,64]{3,2,1,0:T(8,128)(2,1)} reshape(bf16[768,2048]{1,0:T(8,128)(2,1)} %gather_fusion.2) | data formatting | bytes 6291456 | tf_op jit(solution)/shard_map/jit(_take)/gather | solution.py:41
  129.5 93.8 %while.10 = (s32[]{:T(128)}, f32[24,32,256]{2,1,0:T(8,128)S(1)}, s32[24,16]{1,0:T(8,128)S(1)}, bf16[72,32,256]{2,1,0:T(8,128)(2,1)S(1)}, f32[24,3,256]{2,0,1:T(8...) while((s32[]{:T(128)}, f32[24,32,256]{2,1,0:T(8,128)S(1)}, ...), condition=%wide.region_1.2_spmd, body=%wide.region_0.1_spmd.sunk | while | flops 78787744 | bytes 1276569 | solution.py:120
  131.6 1.8 fusion.106
  135.5 1.8 fusion.106
  139.4 1.8 fusion.106
  143.3 1.8 fusion.106
  147.3 1.8 fusion.106
  151.2 1.8 fusion.106
  155.1 1.8 fusion.106
  159.0 1.8 fusion.106
  163.0 1.8 fusion.106
  166.9 1.8 fusion.106
  170.8 1.8 fusion.106
  174.8 1.8 fusion.106
  178.7 1.8 fusion.106
  182.6 1.8 fusion.106
  186.6 1.8 fusion.106
  190.5 1.8 fusion.106
  194.4 1.8 fusion.106
  198.2 1.8 fusion.106
  202.1 1.8 fusion.106
  206.0 1.8 fusion.106
  209.8 1.8 fusion.106
  213.7 1.8 fusion.106
  217.6 1.8 fusion.106
  221.4 1.8 fusion.106
  223.3 8.7 %fusion.27 = bf16[24,4,8,256]{3,2,1,0:T(8,128)(2,1)S(1)} fusion(f32[24,32,256]{2,1,0:T(8,128)S(1)} %get-tuple-element.42, bf16[24,64,256]{2,1,0:T(8,128)(2,1)S(1)} %copy-done, f32[24,32,64]{2,1,0:T(8,128)} %bitcast.143, bf16[24,32,64,64]{3,2,1,0:T(8,128)(2,1)} %reshape.240, bf16[24,32,32,64]{3,2,1,0:T(8,128)(2,1)} %gather.27, ...), kind=kOutput, calls=%fused_computation.49 | convolution fusion | flops 230129664 | bytes 11602176 | tf_op jit(solution)/shard_map/brk,bkp->brp/dot_general | solution.py:138
  (345 shorter events, 61.2 us)
Async XLA Ops:
  0.0 2.6 %copy-start = (bf16[24,64,256]{2,1,0:T(8,128)(2,1)S(1)}, bf16[24,64,256]{2,1,0:T(8,128)(2,1)}, u32[]{:S(2)}) copy-start(bf16[24,64,256]{2,1,0:T(8,128)(2,1)} %param.16) | copy-start | bytes 2359300
  0.0 44.1 %copy-start.1 = (bf16[32,6144]{1,0:T(8,128)(2,1)S(1)}, bf16[32,6144]{1,0:T(8,128)(2,1)}, u32[]{:S(2)}) copy-start(bf16[32,6144]{1,0:T(8,128)(2,1)} %param.14) | copy-start | bytes 1179652
  0.0 44.1 %copy-start.10 = (s32[6,32]{1,0:T(8,128)S(1)}, s32[6,32]{1,0:T(8,128)}, u32[]{:S(2)}) copy-start(s32[6,32]{1,0:T(8,128)} %param.25) | copy-start | bytes 2308
  0.0 44.2 %copy-start.8 = (s32[24,16]{0,1:T(8,128)S(1)}, s32[24,16]{0,1:T(8,128)}, u32[]{:S(2)}) copy-start(s32[24,16]{0,1:T(8,128)} %param.19) | copy-start | bytes 4612
  0.0 44.9 %copy-start.7 = (s32[12,32]{1,0:T(8,128)S(1)}, s32[12,32]{1,0:T(8,128)}, u32[]{:S(2)}) copy-start(s32[12,32]{1,0:T(8,128)} %param.24) | copy-start | bytes 4612
  1.3 45.0 %copy-start.5 = (s32[24,32]{1,0:T(8,128)S(1)}, s32[24,32]{1,0:T(8,128)}, u32[]{:S(2)}) copy-start(s32[24,32]{1,0:T(8,128)} %param.23) | copy-start | bytes 9220
  2.6 49.9 %copy-start.2 = (bf16[12,2,64,64]{3,2,1,0:T(8,128)(2,1)}, bf16[12,2,64,64]{3,2,1,0:T(8,128)(2,1)S(1)}, u32[]{:S(2)}) copy-start(bf16[12,2,64,64]{3,2,1,0:T(8,128)(2,1)S(1)} %reshape.242) | copy-start | bytes 589828
  11.1 69.1 %collective-permute-start.7 = (bf16[24,2048]{1,0:T(8,128)(2,1)S(1)}, bf16[24,2048]{1,0:T(8,128)(2,1)S(1)}, u32[]{:S(2)}, u32[]{:S(2)}) collective-permute-start(bf16[24,2048]{1,0:T(8,128)(2,1)S(1)} %reshape.296), channel_id=1, source_target_pairs={{4,0},{8,4},{12,8},{16,12},{20,16},{24,20},{28,24},{5,1},{9,5},{13... | collective-permute-start | bytes 294920 | tf_op jit(solution)/shard_map/ppermute | solution.py:21
  15.7 67.6 %collective-permute-start.6 = (bf16[24,2048]{1,0:T(8,128)(2,1)S(1)}, bf16[24,2048]{1,0:T(8,128)(2,1)}, u32[]{:S(2)}, u32[]{:S(2)}) collective-permute-start(bf16[24,2048]{1,0:T(8,128)(2,1)S(1)} %reshape.296), channel_id=1, source_target_pairs={{0,4},{4,8},{8,12},{12,16},{16,20},{20,24},{24,28},{1,5},{5,9},{9,... | collective-permute-start | bytes 294920 | tf_op jit(solution)/shard_map/ppermute | solution.py:19
  25.8 68.5 %collective-permute-start.5 = (bf16[48,2048]{1,0:T(8,128)(2,1)S(1)}, bf16[48,2048]{1,0:T(8,128)(2,1)S(1)}, u32[]{:S(2)}, u32[]{:S(2)}) collective-permute-start(bf16[48,2048]{1,0:T(8,128)(2,1)S(1)} %reshape.294), channel_id=1, source_target_pairs={{4,0},{8,4},{12,8},{16,12},{20,16},{24,20},{28,24},{5,1},{9,5},{13... | collective-permute-start | bytes 589832 | tf_op jit(solution)/shard_map/ppermute | solution.py:21
  28.6 70.0 %collective-permute-start.4 = (bf16[48,2048]{1,0:T(8,128)(2,1)S(1)}, bf16[48,2048]{1,0:T(8,128)(2,1)S(1)}, u32[]{:S(2)}, u32[]{:S(2)}) collective-permute-start(bf16[48,2048]{1,0:T(8,128)(2,1)S(1)} %reshape.294), channel_id=1, source_target_pairs={{0,4},{4,8},{8,12},{12,16},{16,20},{20,24},{24,28},{1,5},{5,9},{9,... | collective-permute-start | bytes 589832 | tf_op jit(solution)/shard_map/ppermute | solution.py:19
  41.2 69.7 %collective-permute-start.3 = (bf16[96,2048]{1,0:T(8,128)(2,1)}, bf16[96,2048]{1,0:T(8,128)(2,1)}, u32[]{:S(2)}, u32[]{:S(2)}) collective-permute-start(bf16[96,2048]{1,0:T(8,128)(2,1)} %all_gather.9), channel_id=1, source_target_pairs={{4,0},{8,4},{12,8},{16,12},{20,16},{24,20},{28,24},{5,1},{9,5},{13... | collective-permute-start | bytes 1179656 | tf_op jit(solution)/shard_map/ppermute | solution.py:21
  62.1 18.0 %copy-start.4 = (bf16[3,6144]{1,0:T(4,128)(2,1)S(1)}, bf16[3,6144]{1,0:T(4,128)(2,1)}, u32[]{:S(2)}) copy-start(bf16[3,6144]{1,0:T(4,128)(2,1)} %param.15) | copy-start | bytes 110596
  80.2 30.8 %collective-permute-start.2 = (bf16[96,2048]{1,0:T(8,128)(2,1)}, bf16[96,2048]{1,0:T(8,128)(2,1)}, u32[]{:S(2)}, u32[]{:S(2)}) collective-permute-start(bf16[96,2048]{1,0:T(8,128)(2,1)} %all_gather.9), channel_id=1, source_target_pairs={{0,4},{4,8},{8,12},{12,16},{16,20},{20,24},{24,28},{1,5},{5,9},{9,... | collective-permute-start | bytes 1179656 | tf_op jit(solution)/shard_map/ppermute | solution.py:19
  83.4 43.3 %collective-permute-start.1 = (bf16[35,6144]{1,0:T(8,128)(2,1)S(1)}, bf16[35,6144]{1,0:T(8,128)(2,1)}, u32[]{:S(2)}, u32[]{:S(2)}) collective-permute-start(bf16[35,6144]{1,0:T(8,128)(2,1)S(1)} %constant_dynamic-update-slice_fusion), channel_id=1, source_target_pairs={{1,0},{2,1},{3,2},{4,3},{5,4},{6,5},{7,6},{8,7},{9,8},{10,9},{11,1... | collective-permute-start | bytes 1290248 | tf_op jit(solution)/shard_map/ppermute | solution.py:21
  90.1 8.5 %copy-start.6 = (s32[1024]{0:T(1024)S(1)}, s32[1024]{0:T(1024)}, u32[]{:S(2)}) copy-start(s32[1024]{0:T(1024)} %pad_clamp_fusion.2) | copy-start | bytes 12292
  94.3 32.4 %collective-permute-start = (bf16[35,6144]{1,0:T(8,128)(2,1)S(1)}, bf16[35,6144]{1,0:T(8,128)(2,1)}, u32[]{:S(2)}, u32[]{:S(2)}) collective-permute-start(bf16[35,6144]{1,0:T(8,128)(2,1)S(1)} %constant_dynamic-update-slice_fusion), channel_id=1, source_target_pairs={{0,1},{1,2},{2,3},{3,4},{4,5},{5,6},{6,7},{7,8},{8,9},{9,10},{10,1... | collective-permute-start | bytes 1290248 | tf_op jit(solution)/shard_map/ppermute | solution.py:19
  101.1 4.3 %copy-start.3 = (bf16[12,2,64,64]{3,2,1,0:T(8,128)(2,1)S(1)}, bf16[12,2,64,64]{3,2,1,0:T(8,128)(2,1)}, u32[]{:S(2)}) copy-start(bf16[12,2,64,64]{3,2,1,0:T(8,128)(2,1)} %copy-done.2) | copy-start | bytes 589828
  101.1 4.3 %copy-start.11 = (bf16[12,32]{1,0:T(8,128)(2,1)S(1)}, bf16[12,32]{1,0:T(8,128)(2,1)}, u32[]{:S(2)}) copy-start(bf16[12,32]{1,0:T(8,128)(2,1)} %get-tuple-element.86) | copy-start | bytes 2308
  101.1 4.3 %copy-start.13 = (pred[12,32]{1,0:T(8,128)(4,1)S(1)}, pred[12,32]{1,0:T(8,128)(4,1)}, u32[]{:S(2)}) copy-start(pred[12,32]{1,0:T(8,128)(4,1)} %get-tuple-element.73) | copy-start | bytes 1156
  101.1 4.3 %copy-start.15 = (f32[6,32,2,64]{3,1,2,0:T(8,128)S(1)}, f32[6,32,2,64]{3,1,2,0:T(8,128)}, u32[]{:S(2)}) copy-start(f32[6,32,2,64]{3,1,2,0:T(8,128)} %fusion.64) | copy-start | bytes 294916
  128.4 1.1 copy-start.14
  129.5 93.8 %copy-start.9 = (bf16[24,32]{1,0:T(8,128)(2,1)S(1)}, bf16[24,32]{1,0:T(8,128)(2,1)}, u32[]{:S(2)}) copy-start(bf16[24,32]{1,0:T(8,128)(2,1)} %get-tuple-element.85) | copy-start | bytes 4612
  129.5 93.8 %copy-start.12 = (pred[24,32]{1,0:T(8,128)(4,1)S(1)}, pred[24,32]{1,0:T(8,128)(4,1)}, u32[]{:S(2)}) copy-start(pred[24,32]{1,0:T(8,128)(4,1)} %get-tuple-element.71) | copy-start | bytes 2308
where the time goes:
time: 236 us; the launch traced here: 233 us
  local copies, waits for them, and re-layouts  92.9 us (39%)
  matrix products  64.2 us (27%)
  starting transfers between devices  25.9 us (11%)
  other arithmetic  24.7 us (10%)
  blocking collectives  22.5 us (10%)
    dot_general x24, matrix products, near_one(): lax.dot_general(gathered, kernel, (((0, 2), (1, 2)), ((), ())), preferred...  43.9 us
    reshape x3, local copies, waits for them, and re-layouts, couple_local(): blocks = matrices.reshape(boxes, slot_count, rank_size, rank_size)  33.1 us
    gather x6, local copies, waits for them, and re-layouts, couple_local(): picked = jnp.take(fetched, local_index.reshape(-1), axis=0)  24.7 us
    all_gather x3, blocking collectives, fetch_group(): joined = lax.all_gather(rows, 'leaf', axis=0, tiled=True)  22.5 us
    mul x24, other arithmetic, near_one(): scale_factor * lax.rsqrt(distance + delta_sq)  15.9 us
    gather x24, local copies, waits for them, and re-layouts, near_one(): source = jnp.take(ext_coords, slot_ids, axis=0)  14.2 us
    ppermute x4, starting transfers between devices, extended_2(): lax.ppermute(tail, axis, [(i, (i + 1) % count) for i in range(ends)])  13.6 us
    gather x24, local copies, waits for them, and re-layouts, near_one(): gathered = jnp.take(ext_values, slot_ids, axis=0)  13.5 us
  transfers between devices with their start and end apart: 8, of which 0 were waited for; matrix products, arithmetic and copies ran while one was open for 31% of the time, Pallas kernels for 0%

commit v1 on v0

v1 whole, which is shorter than its diff:
```python
import functools
import math

import jax
import jax.numpy as jnp
from jax import lax
from jax.experimental import pallas as pl
from jax.experimental.pallas import tpu as pltpu
from jax.sharding import PartitionSpec as P

delta_sq = 0.01
BF = jnp.bfloat16
F32 = jnp.float32
LANES = 128
COORD = 64.0
HALF = 8
UNROLL = 2 * HALF
SMEM = pltpu.SMEM
VMEM = pltpu.VMEM
LAST = (((1,), (1,)), ((), ()))


def dot(a, b):
    return jnp.dot(a, b, preferred_element_type=F32)


def dot_last(a, b):
    return lax.dot_general(a, b, LAST, preferred_element_type=F32)


def swap_halves(x):
    half = x.shape[1] // 2
    return jnp.concatenate([x[:, half:], x[:, :half]], axis=1)


def spread_pair(pair):
    lane = lax.broadcasted_iota(jnp.int32, pair.shape, 1)
    low = lane < pair.shape[1] // 2
    zero = jnp.zeros_like(pair)
    turned = swap_halves(pair)
    first = jnp.concatenate([jnp.where(low, pair, zero), jnp.where(low, zero, turned)], axis=0)
    second = jnp.concatenate([jnp.where(low, turned, zero), jnp.where(low, zero, pair)], axis=0)
    return first, second


def parity_matrix(half, parity, dtype=BF):
    row = lax.broadcasted_iota(jnp.int32, (half, 2 * half), 0)
    col = lax.broadcasted_iota(jnp.int32, (half, 2 * half), 1)
    return jnp.where(col == 2 * row + parity, 1.0, 0.0).astype(dtype)


def rows_by_box(flat):
    half = flat.shape[1] // LANES
    parts = jnp.stack([flat[:, q * LANES : (q + 1) * LANES] for q in range(half)], axis=0)
    return jnp.swapaxes(parts, 0, 1)


def peer(index, step, count):
    return index ^ step if count & (count - 1) == 0 else (step - index) % count


def up_kernel(
    members,
    near_smem,
    list0,
    list1,
    list2,
    src,
    basis,
    tr1,
    tr2,
    level_out,
    own_out,
    halo_out,
    count_out,
    tl0,
    tl1,
    tl2,
):
    leaves, slots = near_smem.shape
    rank = basis.shape[1]
    width = basis.shape[2]
    half = rank // 2
    boxes = leaves + leaves // 2 + leaves // 4
    dom = lax.axis_index("dom")
    leaf = lax.axis_index("leaf")

    zero_box = 3 * members * boxes
    offset = 0
    for lst, out, n in ((list0, tl0, leaves), (list1, tl1, leaves // 2), (list2, tl2, leaves // 4)):
        entry = lst[...]
        rel = entry - (dom - 1) * (members * n)
        unit = jnp.zeros_like(rel)
        for t in range(1, 3 * members):
            unit = unit + (rel >= t * n).astype(jnp.int32)
        local = rel - unit * n
        ring = (unit >= members).astype(jnp.int32) + (unit >= 2 * members).astype(jnp.int32)
        lf = unit - ring * members
        if members & (members - 1) == 0:
            place = lf ^ leaf
        else:
            place = lf + leaf
            place = place - jnp.where(place >= members, members, 0)
        spot = (ring * members + place) * boxes + offset + local
        out[...] = jnp.where(entry >= 0, spot, zero_box)
        offset += n

    first = (dom * members + leaf) * leaves

    def scan(b, carry):
        po, ph = carry
        for t in range(slots):
            e = near_smem[b, t]
            rel = e - first
            valid = e >= 0
            own = valid & (rel >= 0) & (rel < leaves)
            halo = valid & jnp.logical_not(own)
            own_out[po] = b * 128 + rel
            halo_out[ph] = b * 128 + jnp.where(rel < 0, rel + leaves, rel)
            po = po + own.astype(jnp.int32)
            ph = ph + halo.astype(jnp.int32)
        return po, ph

    for t in range(HALF):
        own_out[t] = leaves * 128
        halo_out[t] = leaves * 128
    po, ph = lax.fori_loop(0, leaves, scan, (jnp.int32(HALF), jnp.int32(HALF)))
    for t in range(UNROLL + HALF):
        own_out[po + t] = leaves * 128
        halo_out[ph + t] = leaves * 128
    count_out[0] = (po + UNROLL - 1) // UNROLL
    count_out[1] = (ph + UNROLL - 1) // UNROLL

    par = [parity_matrix(half, 0), parity_matrix(half, 1)]

    def raise_level(pairs, mats):
        found = []
        for p, pair in enumerate(pairs):
            e0, e1 = spread_pair(pair)
            wide = jnp.concatenate([e0, e1], axis=1)
            mat = jnp.concatenate([mats[2 * p], mats[2 * p + 1]], axis=1)
            found.append(dot_last(wide, mat).astype(BF))
        rhs = pairs[0].shape[0]
        up = [jnp.concatenate([f[c * rhs : (c + 1) * rhs] for f in found], axis=0) for c in range(2)]
        nat = dot(up[0], par[0]) + dot(up[1], par[1])
        nat = nat.astype(BF)
        return [
            jnp.concatenate(
                [nat[2 * p * rhs : (2 * p + 1) * rhs], nat[(2 * p + 1) * rhs : (2 * p + 2) * rhs]],
                axis=1,
            )
            for p in range(len(pairs) // 2)
        ]

    pairs0 = []
    for p in range(leaves // 2):
        parts = [
            dot_last(src[:, b * width : (b + 1) * width], basis[b]) for b in (2 * p, 2 * p + 1)
        ]
        pairs0.append(jnp.concatenate(parts, axis=1).astype(BF))
    pairs1 = raise_level(pairs0, rows_by_box(tr1[...]))
    pairs2 = raise_level(pairs1, rows_by_box(tr2[...]))
    for p, pair in enumerate(pairs0 + pairs1 + pairs2):
        level_out[p] = pair


def features(points, raw, target):
    x = points.astype(F32) * COORD
    square = x * x
    rest = square[0:1] + square[1:2] + square[2:3]
    lanes = x.shape[1]
    if target:
        rest = rest + delta_sq * COORD * COORD
        raw[0:3, :] = -2.0 * x
        at_parts, at_ones = 3, 6
    else:
        raw[0:3, :] = x
        at_parts, at_ones = 6, 3
    for k in range(3):
        part = rest.astype(BF).astype(F32)
        raw[at_parts + k : at_parts + k + 1, :] = part
        rest = rest - part
    raw[at_ones : at_ones + 3, :] = jnp.ones((3, lanes), F32)
    raw[9:16, :] = jnp.zeros((7, lanes), F32)


def target_features(points, raw, ft, width):
    features(points, raw, True)
    count = points.shape[1] // width
    for b in range(count):
        ft[b, 0:16, :] = raw[:, b * width : (b + 1) * width].astype(BF)
        ft[b, 16:, :] = jnp.zeros((LANES - 16, width), BF)
    ft[count] = jnp.zeros((LANES, width), BF)


def source_features(points, raw, fs, base, width):
    features(points, raw, False)
    for b in range(points.shape[1] // width):
        rows = raw[:, b * width : (b + 1) * width]
        rows = jnp.concatenate([rows, jnp.zeros((LANES - 16, width), F32)], axis=0)
        fs[base + b * width : base + (b + 1) * width, :] = jnp.transpose(rows).astype(BF)


def pair_loop(count, lst, ft, fs, values, acc, held, width):
    def block(code):
        b = code // 128
        g = code % 128
        near = dot(fs[pl.ds(pl.multiple_of(g * width, width), width), :], ft[b])
        return lax.rsqrt(near).astype(BF)

    def add(code, kernel):
        b = code // 128
        g = code % 128
        acc[b] += dot(values[:, pl.ds(pl.multiple_of(g * width, width), width)], kernel)

    held[...] = jnp.zeros_like(held)

    def body(n, carry):
        for h in range(2):
            for u in range(HALF):
                at = n * UNROLL + h * HALF + u
                add(lst[at], held[(1 - h) * HALF + u])
                held[h * HALF + u] = block(lst[at + HALF])
        return carry

    lax.fori_loop(0, count, body, 0)


def near_own_kernel(width, count, lst, points, values, acc, raw, ft, fs, held):
    acc[...] = jnp.zeros_like(acc)
    target_features(points[...], raw, ft, width)
    source_features(points[...], raw, fs, 0, width)
    pair_loop(count[0], lst, ft, fs, values, acc, held, width)


def near_halo_kernel(width, count, lst, points, left, right, acc_in, acc, raw, ft, fs, held, values):
    rhs = left.shape[0] - 3
    span = left.shape[1]
    acc[...] = acc_in[...]
    target_features(points[...], raw, ft, width)
    for k, side in enumerate((left, right)):
        source_features(side[rhs:, :], raw, fs, k * span, width)
        values[:, k * span : (k + 1) * span] = side[:rhs, :]
    pair_loop(count[1], lst, ft, fs, values, acc, held, width)


CHUNK = 3


def far_kernel(
    factor,
    tl0,
    tl1,
    tl2,
    lv_left,
    lv_own,
    lv_right,
    tr1,
    tr2,
    basis,
    acc,
    cp0,
    cp1,
    cp2,
    out,
    wide,
    mats,
    found,
    sems,
):
    members, pairs = lv_own.shape[0], lv_own.shape[1]
    boxes = 2 * pairs
    leaves, rank, width = basis.shape
    half = rank // 2
    rhs = lv_own.shape[2]
    slots = tl0.shape[1]
    levels = ((cp2, tl2, leaves + leaves // 2), (cp1, tl1, leaves), (cp0, tl0, 0))

    copies = []
    for cp, tl, base in levels:
        for k in range(cp.shape[0] // CHUNK):
            at = base + k * CHUNK
            copies.append(
                pltpu.make_async_copy(
                    cp.at[pl.ds(k * CHUNK, CHUNK)], mats.at[pl.ds(at, CHUNK)], sems.at[at // CHUNK]
                )
            )
    for copy in copies:
        copy.start()

    wide[3 * members * boxes] = jnp.zeros((2 * rhs, LANES), BF)
    for s, lv in enumerate((lv_left, lv_own, lv_right)):

        def widen(m, carry):
            for p in range(pairs):
                e0, e1 = spread_pair(lv[m, p])
                at = (s * members + m) * boxes + 2 * p
                wide[at] = e0
                wide[at + 1] = e1
            return carry

        lax.fori_loop(0, members, widen, 0)

    for cp, tl, base in levels:

        def chunk(n, carry):
            at = base + n * CHUNK
            pltpu.make_async_copy(
                cp.at[pl.ds(n * CHUNK, CHUNK)], mats.at[pl.ds(at, CHUNK)], sems.at[at // CHUNK]
            ).wait()
            rows = [rows_by_box(mats[at + u]) for u in range(CHUNK)]
            sums = []
            for u in range(CHUNK):
                total = None
                for s in range(0, slots, 2):
                    co = jnp.concatenate(
                        [wide[tl[n * CHUNK + u, s]], wide[tl[n * CHUNK + u, s + 1]]], axis=1
                    )
                    mat = jnp.concatenate([rows[u][s], rows[u][s + 1]], axis=1)
                    term = dot_last(co, mat)
                    total = term if total is None else total + term
                sums.append(total)
            for u in range(CHUNK):
                found[at + u] = sums[u]
            return carry

        lax.fori_loop(0, cp.shape[0] // CHUNK, chunk, 0)

    par = [parity_matrix(half, 0), parity_matrix(half, 1)]

    def natural(base, n):
        total = None
        for c in range(2):
            part = found[base : base + n, c * rhs : (c + 1) * rhs, :].reshape(n * rhs, half)
            high = part.astype(BF)
            low = (part - high.astype(F32)).astype(BF)
            term = dot(high, par[c]) + dot(low, par[c])
            total = term if total is None else total + term
        return total

    def lower(far, upper, mat, n):
        result = []
        for b in range(n):
            for c in range(2):
                x = dot(upper[b], mat[2 * b + c])
                spread = x[:rhs, :rank] + x[rhs:, rank:]
                at = (2 * b + c) * rhs
                result.append((far[at : at + rhs] + spread).astype(BF))
        return result

    top = leaves // 4
    base2 = leaves + leaves // 2
    down_two = [found[base2 + b].astype(BF) for b in range(top)]
    far_one = natural(leaves, leaves // 2)
    far_zero = natural(0, leaves)
    down_one = lower(far_one, down_two, rows_by_box(tr2[...]), top)
    stacked = jnp.concatenate(down_one, axis=0)
    split = [dot_last(stacked, par[c]).astype(BF) for c in range(2)]
    down_one_split = [
        jnp.concatenate([split[c][b * rhs : (b + 1) * rhs] for c in range(2)], axis=0)
        for b in range(leaves // 2)
    ]
    down_zero = lower(far_zero, down_one_split, rows_by_box(tr1[...]), leaves // 2)
    for b in range(leaves):
        total = acc[b] * factor + dot(down_zero[b], basis[b])
        out[:, b * width : (b + 1) * width] = total.astype(BF)


def params(megabytes):
    return pltpu.CompilerParams(vmem_limit_bytes=megabytes << 20)


def cost(flops, nbytes):
    return pl.CostEstimate(flops=flops, bytes_accessed=nbytes, transcendentals=0)


def shards(
    sources,
    points,
    basis,
    transfer_one,
    transfer_two,
    near_list,
    couple_zero,
    couple_one,
    couple_two,
    list_zero,
    list_one,
    list_two,
):
    rhs, span = sources.shape
    leaves, rank, width = basis.shape
    slots = near_list.shape[1]
    members = lax.axis_size("leaf")
    groups = lax.axis_size("dom")
    devices = members * groups
    pairs = (leaves + leaves // 2 + leaves // 4) // 2
    boxes = 2 * pairs
    half = rank // 2
    smem = pl.BlockSpec(memory_space=SMEM)
    vmem = pl.BlockSpec(memory_space=VMEM)
    hbm = pl.BlockSpec(memory_space=pl.ANY)
    sds = jax.ShapeDtypeStruct
    both = ("dom", "leaf")

    stacked = jnp.concatenate([sources, points], axis=0)
    left = lax.ppermute(stacked, both, [(i, i + 1) for i in range(devices - 1)])
    right = lax.ppermute(stacked, both, [(i + 1, i) for i in range(devices - 1)])

    list_size = leaves * slots + UNROLL + 2 * HALF
    level, own_pairs, halo_pairs, counts, tl0, tl1, tl2 = pl.pallas_call(
        functools.partial(up_kernel, members),
        name="upward",
        in_specs=[smem] + [vmem] * 7,
        out_specs=[vmem, smem, smem, smem, vmem, vmem, vmem],
        out_shape=[
            sds((pairs, rhs, 2 * rank), BF),
            sds((list_size,), jnp.int32),
            sds((list_size,), jnp.int32),
            sds((2,), jnp.int32),
            sds(list_zero.shape, jnp.int32),
            sds(list_one.shape, jnp.int32),
            sds(list_two.shape, jnp.int32),
        ],
        compiler_params=params(24),
        cost_estimate=cost(100_000_000, 10_000_000),
    )(near_list, list_zero, list_one, list_two, sources, basis, transfer_one, transfer_two)

    pieces = [level]
    for step in range(1, members):
        pieces.append(
            lax.ppermute(level, "leaf", [(i, peer(i, step, members)) for i in range(members)])
        )

    acc_shape = sds((leaves + 1, rhs, width), F32)
    near_scratch = [
        pltpu.VMEM((16, span), F32),
        pltpu.VMEM((leaves + 1, LANES, width), BF),
    ]
    acc = pl.pallas_call(
        functools.partial(near_own_kernel, width),
        name="near_own",
        in_specs=[smem, smem, vmem, vmem],
        out_specs=vmem,
        out_shape=acc_shape,
        scratch_shapes=near_scratch
        + [pltpu.VMEM((span, LANES), BF), pltpu.VMEM((UNROLL, width, width), BF)],
        compiler_params=params(32),
        cost_estimate=cost(5_000_000_000, 30_000_000),
    )(counts, own_pairs, points, sources)

    joined = jnp.stack(pieces, axis=0)
    acc, halo_pairs, joined = lax.optimization_barrier((acc, halo_pairs, joined))
    lv_left = lax.ppermute(joined, "dom", [(i, i + 1) for i in range(groups - 1)])
    lv_right = lax.ppermute(joined, "dom", [(i + 1, i) for i in range(groups - 1)])

    acc = pl.pallas_call(
        functools.partial(near_halo_kernel, width),
        name="near_halo",
        in_specs=[smem, smem, vmem, vmem, vmem, vmem],
        out_specs=vmem,
        out_shape=acc_shape,
        scratch_shapes=near_scratch
        + [
            pltpu.VMEM((2 * span, LANES), BF),
            pltpu.VMEM((UNROLL, width, width), BF),
            pltpu.VMEM((rhs, 2 * span), BF),
        ],
        compiler_params=params(32),
        cost_estimate=cost(5_000_000_000, 30_000_000),
    )(counts, halo_pairs, points, left, right, acc)

    factor = COORD / math.sqrt(slots * width)
    return pl.pallas_call(
        functools.partial(far_kernel, factor),
        name="far",
        in_specs=[smem] * 3 + [vmem] * 7 + [hbm] * 3,
        out_specs=vmem,
        out_shape=sds((rhs, span), BF),
        scratch_shapes=[
            pltpu.VMEM((3 * members * boxes + 1, 2 * rhs, LANES), BF),
            pltpu.VMEM((boxes,) + couple_zero.shape[1:], BF),
            pltpu.VMEM((boxes, 2 * rhs, half), F32),
            pltpu.SemaphoreType.DMA((boxes // CHUNK,)),
        ],
        compiler_params=params(60),
        cost_estimate=cost(5_000_000_000, 30_000_000),
    )(
        tl0,
        tl1,
        tl2,
        lv_left,
        joined,
        lv_right,
        transfer_one,
        transfer_two,
        basis,
        acc,
        couple_zero,
        couple_one,
        couple_two,
    )


def solution(mesh):
    row = P(None, ("dom", "leaf"))
    two = P(("dom", "leaf"), None)
    three = P(("dom", "leaf"), None, None)
    placed = (row, row, three, two, two, two, three, three, three, two, two, two)
    return jax.shard_map(shards, mesh=mesh, in_specs=placed, out_specs=row, check_vma=False)
```

time: 236 us -> 73.2 us (0.31); the launches traced: 233 us -> 72.4 us
  local copies, waits for them, and re-layouts: 92.9 us -> 11.5 us
  matrix products: 64.2 us -> 0 us
  Pallas kernels: 0 us -> 43 us
  other arithmetic: 24.7 us -> 0.09 us
  blocking collectives: 22.5 us -> 0 us
  starting transfers between devices: 25.9 us -> 15 us
  waiting for transfers between devices: 0.02 us -> 2.65 us
    dot_general x30 -> x0, matrix products: 64.2 us -> none  [the longest x24 43.9 us: near_one(): lax.dot_general(gathered, kernel, (((0, 2), (1, 2)), ((), ())), preferred...]
    gather x54 -> x0, local copies, waits for them, and re-layouts: 52.5 us -> none  [the longest x6 24.7 us: couple_local(): picked = jnp.take(fetched, local_index.reshape(-1), axis=0)]
    pallas_call x0 -> x4, Pallas kernels: none -> 43 us  [the longest x1 13.9 us: shards(): pl.pallas_call(functools.partial(far_kernel, factor), name='far', in_spec...]
    reshape x9 -> x0, local copies, waits for them, and re-layouts: 36.1 us -> none  [the longest x3 33.1 us: couple_local(): blocks = matrices.reshape(boxes, slot_count, rank_size, rank_size)]
    all_gather x3 -> x0, blocking collectives: 22.5 us -> none  [fetch_group(): joined = lax.all_gather(rows, 'leaf', axis=0, tiled=True)]
    mul x24 -> x0, other arithmetic: 15.9 us -> none  [near_one(): scale_factor * lax.rsqrt(distance + delta_sq)]
    ppermute x8 -> x7, starting transfers between devices: 25.9 us -> 15 us  [the longest x1 4.02 us: shards(): left = lax.ppermute(stacked, both, [(i, i + 1) for i in range(devices - 1)])]
    unnamed x39 -> x36, local copies, waits for them, and re-layouts: 1.41 us -> 10.6 us
  transfers between devices with their start and end apart: 8 -> 7, of which waited for: 0 -> 1; matrix products, arithmetic and copies ran while one was open for 31% -> 1% of each run, Pallas kernels for 0% -> 33%
where the time goes in v1:
time: 73.2 us; the launch traced here: 72.4 us
  Pallas kernels  43 us (59%)
  starting transfers between devices  15 us (20%)
  local copies, waits for them, and re-layouts  11.5 us (16%)
  waiting for transfers between devices  2.65 us (4%)
    pallas_call x1, Pallas kernels, shards(): pl.pallas_call(functools.partial(far_kernel, factor), name='far', in_spec...  13.9 us
    pallas_call x1, Pallas kernels, shards(): pl.pallas_call(functools.partial(near_halo_kernel, width), name='near_hal...  12.2 us
    pallas_call x1, Pallas kernels, shards(): pl.pallas_call(functools.partial(near_own_kernel, width), name='near_own'...  11.7 us
    unnamed x36, local copies, waits for them, and re-layouts  10.6 us
    pallas_call x1, Pallas kernels, shards(): pl.pallas_call(functools.partial(up_kernel, members), name='upward', in_s...  5.25 us
    ppermute x1, starting transfers between devices, shards(): left = lax.ppermute(stacked, both, [(i, i + 1) for i in range(devices - 1)])  4.02 us
    ppermute x1, starting transfers between devices, shards(): lax.ppermute(joined, 'dom', [(i, i + 1) for i in range(groups - 1)])  3.1 us
    ppermute x1, starting transfers between devices, shards(): lax.ppermute(joined, 'dom', [(i + 1, i) for i in range(groups - 1)])  3.04 us
  transfers between devices with their start and end apart: 7, of which 1 were waited for; matrix products, arithmetic and copies ran while one was open for 1% of the time, Pallas kernels for 33%

profile of v1, /device:TPU:11, one launch (start us, length us, event | category | flops | bytes accessed | tf_op | source)
XLA Modules:
  0.0 72.4 jit_solution(18269646852488238127)
XLA Ops:
  0.0 0.8 %copy.13.near_smem = s32[24,16]{1,0:T(8,128)S(1)} copy(s32[24,16]{0,1:T(8,128)} %param.17) | data formatting | bytes 3072 | tf_op args[5]
  0.8 0.0 copy-start
  0.8 1.0 %copy-done = bf16[32,6144]{1,0:T(8,128)(2,1)S(1)} copy-done((bf16[32,6144]{1,0:T(8,128)(2,1)S(1)}, bf16[32,6144]{1,0:T(8,128)(2,1)}, u32[]{:S(2)}) %copy-start) | copy-done | bytes 393240
  1.8 1.1 %copy-done.2 = bf16[24,64,256]{2,1,0:T(8,128)(2,1)S(1)} copy-done((bf16[24,64,256]{2,1,0:T(8,128)(2,1)S(1)}, bf16[24,64,256]{2,1,0:T(8,128)(2,1)}, u32[]{:S(2)}) %copy-start.2) | copy-done | bytes 786456
  2.9 0.0 copy-start.3
  2.9 0.9 %copy-done.3 = bf16[24,4096]{1,0:T(8,128)(2,1)S(1)} copy-done((bf16[24,4096]{1,0:T(8,128)(2,1)S(1)}, bf16[24,4096]{1,0:T(8,128)(2,1)}, u32[]{:S(2)}) %copy-start.3) | copy-done | bytes 196632
  3.8 0.0 copy-start.4
  3.8 0.9 %copy-done.4 = bf16[12,4096]{1,0:T(8,128)(2,1)S(1)} copy-done((bf16[12,4096]{1,0:T(8,128)(2,1)S(1)}, bf16[12,4096]{1,0:T(8,128)(2,1)}, u32[]{:S(2)}) %copy-start.4) | copy-done | bytes 98328
  4.7 0.7 copy-done.7
  5.4 0.7 copy-done.8
  6.1 0.7 copy-done.9
  6.8 5.3 %upward.1 = (bf16[21,32,128]{2,1,0:T(8,128)(2,1)S(1)}, s32[416]{0:T(512)S(1)}, s32[416]{0:T(512)S(1)}, s32[2]{0:T(128)S(1)}, s32[24,32]{1,0:T(8,128)S(1)}, /*index=5*/s32[12,32]{1,0:T(8,128)S(1)}, s32[6,32]{1,0:T(8,128)S(1)}) custom-call(s32[24,16]{1,0:T(8,128)S(1)} %copy.13.near_smem, s32[24,32]{1,0:T(8,128)S(1)} %copy-done.7, s32[12,32]{1,0:T(8,128)S(1)} %copy-done.8, ...), custom_call_target="tpu_custom_call" | custom-call | flops 100000000 | bytes 10000000 | tf_op jit(solution)/shard_map/upward/pallas_call | solution.py:411
  12.1 0.0 copy-start.10
  12.1 0.0 copy-start.11
  12.1 0.0 copy-start.12
  12.1 1.3 %collective-permute-start.2 = (bf16[21,32,128]{2,1,0:T(8,128)(2,1)S(1)}, bf16[21,32,128]{2,1,0:T(8,128)(2,1)S(1)}, u32[]{:S(2)}, u32[]{:S(2)}) collective-permute-start(bf16[21,32,128]{2,1,0:T(8,128)(2,1)S(1)} %get-tuple-element.21), channel_id=1, source_target_pairs={{0,3},{1,2},{2,1},{3,0},{4,7},{5,6},{6,5},{7,4},{8,11},{9,10},{10,... | collective-permute-start | bytes 516104 | tf_op jit(solution)/shard_map/ppermute | solution.py:432
  13.4 0.2 collective-permute-start.1
  13.6 1.2 %collective-permute-start = (bf16[21,32,128]{2,1,0:T(8,128)(2,1)S(1)}, bf16[21,32,128]{2,1,0:T(8,128)(2,1)S(1)}, u32[]{:S(2)}, u32[]{:S(2)}) collective-permute-start(bf16[21,32,128]{2,1,0:T(8,128)(2,1)S(1)} %get-tuple-element.21), channel_id=1, source_target_pairs={{0,1},{1,0},{2,3},{3,2},{4,5},{5,4},{6,7},{7,6},{8,9},{9,8},{10,11... | collective-permute-start | bytes 516104 | tf_op jit(solution)/shard_map/ppermute | solution.py:432
  14.9 0.8 %constant_dynamic-update-slice_fusion = bf16[35,6144]{1,0:T(8,128)(2,1)S(1)} fusion(bf16[35,6144]{1,0:T(8,128)(2,1)S(1)} %constant_dynamic-update-slice_fusion.1, bf16[3,6144]{1,0:T(4,128)(2,1)} %points.3), kind=kLoop, calls=%fused_computation.1 | loop fusion | bytes 86016 | tf_op jit(solution)/shard_map/concatenate | solution.py:406
  15.7 2.2 %collective-permute-start.6 = (bf16[35,6144]{1,0:T(8,128)(2,1)S(1)}, bf16[35,6144]{1,0:T(8,128)(2,1)S(1)}, u32[]{:S(2)}, u32[]{:S(2)}) collective-permute-start(bf16[35,6144]{1,0:T(8,128)(2,1)S(1)} %constant_dynamic-update-slice_fusion), channel_id=1, source_target_pairs={{1,0},{2,1},{3,2},{4,3},{5,4},{6,5},{7,6},{8,7},{9,8},{10,9},{11,1... | collective-permute-start | bytes 1290248 | tf_op jit(solution)/shard_map/ppermute | solution.py:408
  17.9 4.0 %collective-permute-start.5 = (bf16[35,6144]{1,0:T(8,128)(2,1)S(1)}, bf16[35,6144]{1,0:T(8,128)(2,1)S(1)}, u32[]{:S(2)}, u32[]{:S(2)}) collective-permute-start(bf16[35,6144]{1,0:T(8,128)(2,1)S(1)} %constant_dynamic-update-slice_fusion), channel_id=1, source_target_pairs={{0,1},{1,2},{2,3},{3,4},{4,5},{5,6},{6,7},{7,8},{8,9},{9,10},{10,1... | collective-permute-start | bytes 1290248 | tf_op jit(solution)/shard_map/ppermute | solution.py:407
  21.9 0.0 copy-done.10
  21.9 0.0 copy-done.11
  21.9 0.0 copy-done.12
  21.9 0.0 copy-start.1
  21.9 1.0 %copy-done.1 = bf16[32,6144]{1,0:T(8,128)(2,1)S(1)} copy-done((bf16[32,6144]{1,0:T(8,128)(2,1)S(1)}, bf16[32,6144]{1,0:T(8,128)(2,1)}, u32[]{:S(2)}) %copy-start.1) | copy-done | bytes 393240
  22.9 0.8 %copy-done.5 = bf16[3,6144]{1,0:T(4,128)(2,1)S(1)} copy-done((bf16[3,6144]{1,0:T(4,128)(2,1)S(1)}, bf16[3,6144]{1,0:T(4,128)(2,1)}, u32[]{:S(2)}) %copy-start.5) | copy-done | bytes 36888
  23.7 11.7 %near_own.1.acc_in = f32[25,32,256]{2,1,0:T(8,128)S(1)} custom-call(s32[2]{0:T(128)S(1)} %get-tuple-element.18.count, s32[416]{0:T(512)S(1)} %get-tuple-element.19.lst, bf16[3,6144]{1,0:T(4,128)(2,1)S(1)} %copy-done.5, bf16[32,6144]{1,0:T(8,128)(2,1)S(1)} %copy-done.1), custom_call_target="tpu_custom_call" | custom-call | flops 5000000000 | bytes 30000000 | tf_op jit(solution)/shard_map/near_own/pallas_call | solution.py:440
  35.4 0.0 collective-permute-done.2
  35.4 0.0 collective-permute-done.1
  35.4 0.0 collective-permute-done
  35.4 0.1 pad_maximum_fusion.lv_own
  35.5 0.0 copy-start.14
  35.5 3.0 %collective-permute-start.4 = (bf16[4,21,32,128]{3,2,1,0:T(8,128)(2,1)S(1)}, bf16[4,21,32,128]{3,2,1,0:T(8,128)(2,1)S(1)}, u32[]{:S(2)}, u32[]{:S(2)}) collective-permute-start(bf16[4,21,32,128]{3,2,1,0:T(8,128)(2,1)S(1)} %pad_maximum_fusion.lv_own), channel_id=1, source_target_pairs={{4,0},{8,4},{12,8},{16,12},{20,16},{24,20},{28,24},{5,1},{9,5},{13... | collective-permute-start | bytes 2064392 | tf_op jit(solution)/shard_map/ppermute | solution.py:455
  38.6 3.1 %collective-permute-start.3 = (bf16[4,21,32,128]{3,2,1,0:T(8,128)(2,1)S(1)}, bf16[4,21,32,128]{3,2,1,0:T(8,128)(2,1)S(1)}, u32[]{:S(2)}, u32[]{:S(2)}) collective-permute-start(bf16[4,21,32,128]{3,2,1,0:T(8,128)(2,1)S(1)} %pad_maximum_fusion.lv_own), channel_id=1, source_target_pairs={{0,4},{4,8},{8,12},{12,16},{16,20},{20,24},{24,28},{1,5},{5,9},{9,... | collective-permute-start | bytes 2064392 | tf_op jit(solution)/shard_map/ppermute | solution.py:454
  41.7 0.0 collective-permute-done.6.right
  41.7 2.6 %collective-permute-done.5.left = bf16[35,6144]{1,0:T(8,128)(2,1)S(1)} collective-permute-done((bf16[35,6144]{1,0:T(8,128)(2,1)S(1)}, bf16[35,6144]{1,0:T(8,128)(2,1)S(1)}, u32[]{:S(2)}, u32[]{:S(2)}) %collective-permute-start.5) | collective-permute-done | bytes 430112 | tf_op jit(solution)/shard_map/ppermute | solution.py:407
  44.3 0.0 copy-done.6
  44.3 12.2 %near_halo.1.acc = f32[25,32,256]{2,1,0:T(8,128)S(1)} custom-call(s32[2]{0:T(128)S(1)} %get-tuple-element.18.count, s32[416]{0:T(512)S(1)} %get-tuple-element.23.lst, bf16[3,6144]{1,0:T(4,128)(2,1)S(1)} %copy-done.6, bf16[35,6144]{1,0:T(8,128)(2,1)S(1)} %collective-permute-done.5.left, bf16[35,6144]{1,0:T(8,128)(2,1)S(1)} %collective-permute-done.6.right, ...), custom_call_target="tpu_custom_call" | custom-call | flops 5000000000 | bytes 30000000 | tf_op jit(solution)/shard_map/near_halo/pallas_call | solution.py:457
  56.5 0.0 copy-done.14
  56.5 0.0 copy-start.13
  56.5 0.9 %copy-done.13 = f32[25,32,256]{2,1,0:T(8,128)} copy-done((f32[25,32,256]{2,1,0:T(8,128)}, f32[25,32,256]{2,1,0:T(8,128)S(1)}, u32[]{:S(2)}) %copy-start.13) | copy-done | bytes 819224
  57.4 0.0 collective-permute-done.4.lv_right
  57.4 0.0 collective-permute-done.3.lv_left
  57.4 0.0 copy-start.16
  57.4 0.8 %copy-done.15 = bf16[4,21,32,128]{3,2,1,0:T(8,128)(2,1)} copy-done((bf16[4,21,32,128]{3,2,1,0:T(8,128)(2,1)}, bf16[4,21,32,128]{3,2,1,0:T(8,128)(2,1)S(1)}, u32[]{:S(2)}) %copy-start.15) | copy-done | bytes 688152
  58.3 0.3 copy-done.16
  58.5 13.9 %far.1 = bf16[32,6144]{1,0:T(8,128)(2,1)} custom-call(s32[24,32]{1,0:T(8,128)} %copy-done.10, s32[12,32]{1,0:T(8,128)} %copy-done.11, s32[6,32]{1,0:T(8,128)} %copy-done.12, bf16[4,21,32,128]{3,2,1,0:T(8,128)(2,1)} %copy-done.16, bf16[4,21,32,128]{3,2,1,0:T(8,128)(2,1)} %copy-done.14, bf16[4,21,32,128]{3,2,1,0:T(8,128)(2,1)} %copy-done.15, ...), custom_call_target="tpu_custom_call" | custom-call | flops 5000000000 | bytes 30000000 | tf_op jit(solution)/shard_map/far/pallas_call | solution.py:474
  (8 shorter events, 0.0 us)
Async XLA Ops:
  0.8 1.0 %copy-start = (bf16[32,6144]{1,0:T(8,128)(2,1)S(1)}, bf16[32,6144]{1,0:T(8,128)(2,1)}, u32[]{:S(2)}) copy-start(bf16[32,6144]{1,0:T(8,128)(2,1)} %values.1) | copy-start | bytes 1179652
  1.8 1.1 %copy-start.2 = (bf16[24,64,256]{2,1,0:T(8,128)(2,1)S(1)}, bf16[24,64,256]{2,1,0:T(8,128)(2,1)}, u32[]{:S(2)}) copy-start(bf16[24,64,256]{2,1,0:T(8,128)(2,1)} %basis.3) | copy-start | bytes 2359300
  2.9 0.9 %copy-start.3 = (bf16[24,4096]{1,0:T(8,128)(2,1)S(1)}, bf16[24,4096]{1,0:T(8,128)(2,1)}, u32[]{:S(2)}) copy-start(bf16[24,4096]{1,0:T(8,128)(2,1)} %tr1.3) | copy-start | bytes 589828
  3.8 0.9 %copy-start.4 = (bf16[12,4096]{1,0:T(8,128)(2,1)S(1)}, bf16[12,4096]{1,0:T(8,128)(2,1)}, u32[]{:S(2)}) copy-start(bf16[12,4096]{1,0:T(8,128)(2,1)} %tr2.3) | copy-start | bytes 294916
  4.7 0.7 copy-start.7
  5.4 0.7 copy-start.8
  6.1 0.7 copy-start.9
  12.1 9.8 %copy-start.10 = (s32[24,32]{1,0:T(8,128)}, s32[24,32]{1,0:T(8,128)S(1)}, u32[]{:S(2)}) copy-start(s32[24,32]{1,0:T(8,128)S(1)} %get-tuple-element.15.tl0) | copy-start | bytes 9220
  12.1 9.8 %copy-start.11 = (s32[12,32]{1,0:T(8,128)}, s32[12,32]{1,0:T(8,128)S(1)}, u32[]{:S(2)}) copy-start(s32[12,32]{1,0:T(8,128)S(1)} %get-tuple-element.16.tl1) | copy-start | bytes 4612
  12.1 9.8 %copy-start.12 = (s32[6,32]{1,0:T(8,128)}, s32[6,32]{1,0:T(8,128)S(1)}, u32[]{:S(2)}) copy-start(s32[6,32]{1,0:T(8,128)S(1)} %get-tuple-element.17.tl2) | copy-start | bytes 2308
  12.1 23.3 %collective-permute-start.2 = (bf16[21,32,128]{2,1,0:T(8,128)(2,1)S(1)}, bf16[21,32,128]{2,1,0:T(8,128)(2,1)S(1)}, u32[]{:S(2)}, u32[]{:S(2)}) collective-permute-start(bf16[21,32,128]{2,1,0:T(8,128)(2,1)S(1)} %get-tuple-element.21), channel_id=1, source_target_pairs={{0,3},{1,2},{2,1},{3,0},{4,7},{5,6},{6,5},{7,4},{8,11},{9,10},{10,... | collective-permute-start | bytes 516104 | tf_op jit(solution)/shard_map/ppermute | solution.py:432
  13.4 22.0 %collective-permute-start.1 = (bf16[21,32,128]{2,1,0:T(8,128)(2,1)S(1)}, bf16[21,32,128]{2,1,0:T(8,128)(2,1)S(1)}, u32[]{:S(2)}, u32[]{:S(2)}) collective-permute-start(bf16[21,32,128]{2,1,0:T(8,128)(2,1)S(1)} %get-tuple-element.21), channel_id=1, source_target_pairs={{0,2},{1,3},{2,0},{3,1},{4,6},{5,7},{6,4},{7,5},{8,10},{9,11},{10,... | collective-permute-start | bytes 516104 | tf_op jit(solution)/shard_map/ppermute | solution.py:432
  13.6 21.8 %collective-permute-start = (bf16[21,32,128]{2,1,0:T(8,128)(2,1)S(1)}, bf16[21,32,128]{2,1,0:T(8,128)(2,1)S(1)}, u32[]{:S(2)}, u32[]{:S(2)}) collective-permute-start(bf16[21,32,128]{2,1,0:T(8,128)(2,1)S(1)} %get-tuple-element.21), channel_id=1, source_target_pairs={{0,1},{1,0},{2,3},{3,2},{4,5},{5,4},{6,7},{7,6},{8,9},{9,8},{10,11... | collective-permute-start | bytes 516104 | tf_op jit(solution)/shard_map/ppermute | solution.py:432
  15.7 26.0 %collective-permute-start.6 = (bf16[35,6144]{1,0:T(8,128)(2,1)S(1)}, bf16[35,6144]{1,0:T(8,128)(2,1)S(1)}, u32[]{:S(2)}, u32[]{:S(2)}) collective-permute-start(bf16[35,6144]{1,0:T(8,128)(2,1)S(1)} %constant_dynamic-update-slice_fusion), channel_id=1, source_target_pairs={{1,0},{2,1},{3,2},{4,3},{5,4},{6,5},{7,6},{8,7},{9,8},{10,9},{11,1... | collective-permute-start | bytes 1290248 | tf_op jit(solution)/shard_map/ppermute | solution.py:408
  17.9 26.5 %collective-permute-start.5 = (bf16[35,6144]{1,0:T(8,128)(2,1)S(1)}, bf16[35,6144]{1,0:T(8,128)(2,1)S(1)}, u32[]{:S(2)}, u32[]{:S(2)}) collective-permute-start(bf16[35,6144]{1,0:T(8,128)(2,1)S(1)} %constant_dynamic-update-slice_fusion), channel_id=1, source_target_pairs={{0,1},{1,2},{2,3},{3,4},{4,5},{5,6},{6,7},{7,8},{8,9},{9,10},{10,1... | collective-permute-start | bytes 1290248 | tf_op jit(solution)/shard_map/ppermute | solution.py:407
  21.9 1.0 %copy-start.1 = (bf16[32,6144]{1,0:T(8,128)(2,1)S(1)}, bf16[32,6144]{1,0:T(8,128)(2,1)}, u32[]{:S(2)}) copy-start(bf16[32,6144]{1,0:T(8,128)(2,1)} %values.1) | copy-start | bytes 1179652
  22.9 0.8 %copy-start.5 = (bf16[3,6144]{1,0:T(4,128)(2,1)S(1)}, bf16[3,6144]{1,0:T(4,128)(2,1)}, u32[]{:S(2)}) copy-start(bf16[3,6144]{1,0:T(4,128)(2,1)} %points.3) | copy-start | bytes 110596
  23.7 20.6 %copy-start.6 = (bf16[3,6144]{1,0:T(4,128)(2,1)S(1)}, bf16[3,6144]{1,0:T(4,128)(2,1)}, u32[]{:S(2)}) copy-start(bf16[3,6144]{1,0:T(4,128)(2,1)} %points.3) | copy-start | bytes 110596
  35.5 21.0 %copy-start.14 = (bf16[4,21,32,128]{3,2,1,0:T(8,128)(2,1)}, bf16[4,21,32,128]{3,2,1,0:T(8,128)(2,1)S(1)}, u32[]{:S(2)}) copy-start(bf16[4,21,32,128]{3,2,1,0:T(8,128)(2,1)S(1)} %pad_maximum_fusion.lv_own) | copy-start | bytes 2064388
  35.5 21.9 %collective-permute-start.4 = (bf16[4,21,32,128]{3,2,1,0:T(8,128)(2,1)S(1)}, bf16[4,21,32,128]{3,2,1,0:T(8,128)(2,1)S(1)}, u32[]{:S(2)}, u32[]{:S(2)}) collective-permute-start(bf16[4,21,32,128]{3,2,1,0:T(8,128)(2,1)S(1)} %pad_maximum_fusion.lv_own), channel_id=1, source_target_pairs={{4,0},{8,4},{12,8},{16,12},{20,16},{24,20},{28,24},{5,1},{9,5},{13... | collective-permute-start | bytes 2064392 | tf_op jit(solution)/shard_map/ppermute | solution.py:455
  38.6 18.8 %collective-permute-start.3 = (bf16[4,21,32,128]{3,2,1,0:T(8,128)(2,1)S(1)}, bf16[4,21,32,128]{3,2,1,0:T(8,128)(2,1)S(1)}, u32[]{:S(2)}, u32[]{:S(2)}) collective-permute-start(bf16[4,21,32,128]{3,2,1,0:T(8,128)(2,1)S(1)} %pad_maximum_fusion.lv_own), channel_id=1, source_target_pairs={{0,4},{4,8},{8,12},{12,16},{16,20},{20,24},{24,28},{1,5},{5,9},{9,... | collective-permute-start | bytes 2064392 | tf_op jit(solution)/shard_map/ppermute | solution.py:454
  56.5 0.9 %copy-start.13 = (f32[25,32,256]{2,1,0:T(8,128)}, f32[25,32,256]{2,1,0:T(8,128)S(1)}, u32[]{:S(2)}) copy-start(f32[25,32,256]{2,1,0:T(8,128)S(1)} %near_halo.1.acc) | copy-start | bytes 2457604
  57.4 0.9 %copy-start.15 = (bf16[4,21,32,128]{3,2,1,0:T(8,128)(2,1)}, bf16[4,21,32,128]{3,2,1,0:T(8,128)(2,1)S(1)}, u32[]{:S(2)}) copy-start(bf16[4,21,32,128]{3,2,1,0:T(8,128)(2,1)S(1)} %collective-permute-done.4.lv_right) | copy-start | bytes 2064388
  57.4 1.1 %copy-start.16 = (bf16[4,21,32,128]{3,2,1,0:T(8,128)(2,1)}, bf16[4,21,32,128]{3,2,1,0:T(8,128)(2,1)S(1)}, u32[]{:S(2)}) copy-start(bf16[4,21,32,128]{3,2,1,0:T(8,128)(2,1)S(1)} %collective-permute-done.3.lv_left) | copy-start | bytes 2064388
